TPU v7x, 32 devices: a whole 2x2x4 slice. The times are simulated.
32 devices in a mesh: lane: 8 (over z, core), rec: 4 (over y, x).
Axes of the slice: x: 2, y: 2, z: 4, core: 2. Of those that a mesh axis runs over, the one named last changes fastest.
Arguments:
- waveforms: bfloat16 [128, 16384], P('lane', 'rec'), may hold values from -6 to 6
- patterns: int32 [128, 16384], P('lane', 'rec'), may hold values from 0 to 3
- partners: int32 [128, 8], P('lane'), may hold values from 0 to 127, as said below
- counts: int32 [128], P('lane'), may hold values from 1 to 8, as said below
Outputs:
- responses: float32 [2, 256, 1024], P(None, 'rec', 'lane')
Inputs may be any that keep to these rules, and one draw needn't show every extreme that they name: partners[l, s] is never l; the 8 partners of a lane lie on 8 different indices of lane; of the 128 entries of the lanes of one index of lane, exactly 16 name lanes of each index of lane. `counts`: uneven over lanes and over indices of lane.
All inputs are finite; a program needn't handle non-finite values.
Results may differ from a plain program's by a relative error of at most 0.0003.
Values may be sent and summed in bfloat16 or wider, within the bound.
A program may use at most 64 MiB of HBM per device.

v0:
```python
import math

import jax
import jax.numpy as jnp
from jax import lax
from jax.sharding import PartitionSpec as P

LAGS = 256


BLOCK = 128


def passed_along(block, axis, distance):
    devices = range(lax.axis_size(axis))
    route = [(i - distance, i) for i in devices if i - distance in devices]
    return lax.ppermute(block, axis, route)


def correlate_group(rows, references):
    count, length = rows.shape
    blocks = length // BLOCK
    reach = references.shape[1] - length
    extra = reach // BLOCK
    row_blocks = rows.reshape(count, blocks, BLOCK)
    ref_blocks = references.reshape(count, blocks + extra, BLOCK)
    window = jnp.concatenate(
        [ref_blocks[:, shift_by : shift_by + blocks] for shift_by in range(extra + 1)], axis=2
    )
    cross = jnp.einsum("rbi,rbj->rij", row_blocks, window, preferred_element_type=jnp.float32)
    width = BLOCK + reach
    spread = jnp.pad(cross.reshape(count, BLOCK * width), ((0, 0), (0, BLOCK)))
    skewed = spread.reshape(count, BLOCK, width + 1)
    totals = jnp.sum(skewed, axis=1)
    return totals[:, reach:0:-1]


def correlate(rows, references):
    count = rows.shape[0]
    group = math.gcd(count, 16)
    stacked_rows = rows.reshape(count // group, group, rows.shape[1])
    stacked_refs = references.reshape(count // group, group, references.shape[1])
    result = lax.map(
        lambda paired: correlate_group(paired[0], paired[1]), (stacked_rows, stacked_refs)
    )
    return result.reshape(count, -1)


def request_layout(targets, lane_dev, capacity):
    target_dev = targets // lane_dev
    serial = jnp.arange(targets.shape[0], dtype=jnp.int32)
    earlier = (target_dev[None, :] == target_dev[:, None]) & (serial[None, :] < serial[:, None])
    ranks = jnp.sum(earlier.astype(jnp.int32), axis=1)
    slot_of = target_dev * capacity + ranks
    order = jnp.sum(jnp.where(slot_of[None, :] == serial[:, None], serial[None, :], 0), axis=1)
    return (slot_of, order)


def per_device(waveforms, patterns, partners, counts):
    lane_dev, time_dev = waveforms.shape
    slots = partners.shape[1]
    lane_count = lax.axis_size("lane")
    capacity = lane_dev * slots // lane_count
    total_time = time_dev * lax.axis_size("rec")
    levels = (2 * patterns - 3).astype(jnp.bfloat16)
    rim = passed_along(levels[:, time_dev - LAGS :], "rec", 1)
    extended = jnp.concatenate([rim, levels], axis=1)
    targets = partners.reshape(-1)
    slot_of, order = request_layout(targets, lane_dev, capacity)
    local_index = targets % lane_dev
    send_rows = waveforms[order // slots].reshape(lane_count, capacity, time_dev)
    send_index = local_index[order].reshape(lane_count, capacity)
    rows_in = lax.all_to_all(send_rows, "lane", split_axis=0, concat_axis=0, tiled=True)
    index_in = lax.all_to_all(send_index, "lane", split_axis=0, concat_axis=0, tiled=True)
    sources, taken = index_in.shape
    flat_index = index_in.reshape(-1)
    forward_part = correlate(rows_in.reshape(sources * taken, time_dev), extended[flat_index])
    reply = waveforms[flat_index].reshape(sources, taken, time_dev)
    returned = lax.all_to_all(reply, "lane", split_axis=0, concat_axis=0, tiled=True)
    held = forward_part.reshape(sources, taken, LAGS)
    reverse_rows = returned.reshape(lane_count * capacity, time_dev)[slot_of]
    lane_refs = jnp.repeat(extended, slots, axis=0)
    backward = correlate(reverse_rows, lane_refs)
    valid = (
        (jnp.arange(slots, dtype=jnp.int32)[None, :] < counts[:, None])
        .astype(jnp.float32)
        .reshape(-1)
    )
    scale = (5.0 * total_time) ** (-0.5)
    back = lax.all_to_all(held, "lane", split_axis=0, concat_axis=0, tiled=True)
    forward = back.reshape(lane_count * capacity, LAGS)[slot_of]
    terms = jnp.stack([forward.T, backward.T]) * valid
    summed = lax.psum_scatter(terms, "rec", scatter_dimension=1, tiled=True)
    return summed * scale


def solution(mesh):
    in_specs = (P("lane", "rec"), P("lane", "rec"), P("lane", None), P("lane"))
    out_specs = P(None, "rec", "lane")
    return jax.shard_map(
        per_device, mesh=mesh, in_specs=in_specs, out_specs=out_specs, check_vma=False
    )
```

profile of v0, /device:TPU:0, one launch (start us, length us, event | category | flops | bytes accessed | tf_op | source)
XLA Modules:
  0.0 295.9 jit_solution(17519920170525431032)
XLA Ops:
  9.7 6.3 %all-to-all-start.1 = ((s32[8,1,16]{2,1,0:T(1,128)}), s32[8,1,16]{2,1,0:T(1,128)S(1)}, u32[]{:S(2)}, u32[]{:S(2)}) async-start(s32[8,1,16]{2,1,0:T(1,128)} %bitcast.6), calls=%async_computation.1 | async-start | bytes 8192 | tf_op jit(solution)/shard_map/all_to_all | solution.py:74
  18.2 3.3 %all-to-all-done.1 = s32[8,1,16]{2,1,0:T(1,128)S(1)} async-done(((s32[8,1,16]{2,1,0:T(1,128)}), s32[8,1,16]{2,1,0:T(1,128)S(1)}, u32[]{:S(2)}, u32[]{:S(2)}) %all-to-all-start.1) | async-done | bytes 544 | tf_op jit(solution)/shard_map/all_to_all | solution.py:74
  21.5 3.6 %all-to-all-start = ((bf16[8,16,4096]{2,1,0:T(8,128)(2,1)}), bf16[8,16,4096]{2,1,0:T(8,128)(2,1)S(1)}, u32[]{:S(2)}, u32[]{:S(2)}) async-start(bf16[8,16,4096]{2,1,0:T(8,128)(2,1)} %bitcast.4), calls=%async_computation | async-start | bytes 2097152 | tf_op jit(solution)/shard_map/all_to_all | solution.py:73
  25.1 3.4 %collective-permute-start = (bf16[16,256]{1,0:T(8,128)(2,1)S(1)}, bf16[16,256]{1,0:T(8,128)(2,1)S(1)}, u32[]{:S(2)}, u32[]{:S(2)}) collective-permute-start(bf16[16,256]{1,0:T(8,128)(2,1)S(1)} %slice.72), channel_id=1, source_target_pairs={{0,1},{1,2},{2,3},{4,5},{5,6},{6,7},{8,9},{9,10},{10,11},{12,13},{... | collective-permute-start | bytes 24584 | tf_op jit(solution)/shard_map/ppermute | solution.py:17
  33.7 17.8 %all-to-all-done = bf16[8,16,4096]{2,1,0:T(8,128)(2,1)S(1)} async-done(((bf16[8,16,4096]{2,1,0:T(8,128)(2,1)}), bf16[8,16,4096]{2,1,0:T(8,128)(2,1)S(1)}, u32[]{:S(2)}, u32[]{:S(2)}) %all-to-all-start) | async-done | bytes 1048608 | tf_op jit(solution)/shard_map/all_to_all | solution.py:73
  51.6 4.2 %all-to-all-start.3 = ((bf16[8,16,4096]{2,1,0:T(8,128)(2,1)}), bf16[8,16,4096]{2,1,0:T(8,128)(2,1)}, u32[]{:S(2)}, u32[]{:S(2)}) async-start(bf16[8,16,4096]{2,1,0:T(8,128)(2,1)} %bitcast.14), calls=%async_computation.3 | async-start | bytes 2097152 | tf_op jit(solution)/shard_map/all_to_all | solution.py:79
  56.5 90.3 %while.24 = (s32[]{:T(128)}, f32[8,16,256]{2,1,0:T(8,128)}, bf16[8,16,4096]{2,1,0:T(8,128)(2,1)S(1)}, bf16[8,16,4352]{2,1,0:T(8,128)(2,1)S(1)}, s32[]{:T(128)}, /*index=5*/f32[]{:T(128)}) while((s32[]{:T(128)}, f32[8,16,256]{2,1,0:T(8,128)}, bf16[8,16,4096]{2,1,0:T(8,128)(2,1)S(1)}, bf16[8,16,4352]{2,1,0:T(8,128)(2,1)S(1)}, s32[]{:T(128)}, ...), condition=%wide.region_4.5_spmd, body=%wide.region_2.4_spmd.sunk | while | flops 52293616 | bytes 45015812 | solution.py:43
  59.4 4.6 %reshape.413 = f32[16,128,385]{2,1,0:T(8,128)} reshape(f32[16,49280]{1,0:T(8,128)S(1)} %pad.72) | data formatting | bytes 6307840 | tf_op jit(solution)/shard_map/while/body/eval_jaxpr/reshape | solution.py:33
  70.7 4.6 %reshape.413 = f32[16,128,385]{2,1,0:T(8,128)} reshape(f32[16,49280]{1,0:T(8,128)S(1)} %pad.72) | data formatting | bytes 6307840 | tf_op jit(solution)/shard_map/while/body/eval_jaxpr/reshape | solution.py:33
  75.3 2.9 reduce_sum.54
  82.0 4.6 %reshape.413 = f32[16,128,385]{2,1,0:T(8,128)} reshape(f32[16,49280]{1,0:T(8,128)S(1)} %pad.72) | data formatting | bytes 6307840 | tf_op jit(solution)/shard_map/while/body/eval_jaxpr/reshape | solution.py:33
  86.6 2.9 reduce_sum.54
  93.3 4.6 %reshape.413 = f32[16,128,385]{2,1,0:T(8,128)} reshape(f32[16,49280]{1,0:T(8,128)S(1)} %pad.72) | data formatting | bytes 6307840 | tf_op jit(solution)/shard_map/while/body/eval_jaxpr/reshape | solution.py:33
  97.9 2.9 reduce_sum.54
  104.6 4.6 %reshape.413 = f32[16,128,385]{2,1,0:T(8,128)} reshape(f32[16,49280]{1,0:T(8,128)S(1)} %pad.72) | data formatting | bytes 6307840 | tf_op jit(solution)/shard_map/while/body/eval_jaxpr/reshape | solution.py:33
  115.9 4.6 %reshape.413 = f32[16,128,385]{2,1,0:T(8,128)} reshape(f32[16,49280]{1,0:T(8,128)S(1)} %pad.72) | data formatting | bytes 6307840 | tf_op jit(solution)/shard_map/while/body/eval_jaxpr/reshape | solution.py:33
  120.5 2.9 reduce_sum.54
  127.2 4.6 %reshape.413 = f32[16,128,385]{2,1,0:T(8,128)} reshape(f32[16,49280]{1,0:T(8,128)S(1)} %pad.72) | data formatting | bytes 6307840 | tf_op jit(solution)/shard_map/while/body/eval_jaxpr/reshape | solution.py:33
  131.8 2.9 reduce_sum.54
  138.4 4.6 %reshape.413 = f32[16,128,385]{2,1,0:T(8,128)} reshape(f32[16,49280]{1,0:T(8,128)S(1)} %pad.72) | data formatting | bytes 6307840 | tf_op jit(solution)/shard_map/while/body/eval_jaxpr/reshape | solution.py:33
  146.8 5.0 %all-to-all-start.2 = ((f32[8,16,256]{2,1,0:T(8,128)}), f32[8,16,256]{2,1,0:T(8,128)S(1)}, u32[]{:S(2)}, u32[]{:S(2)}) async-start(f32[8,16,256]{2,1,0:T(8,128)} %get-tuple-element.111), calls=%async_computation.2 | async-start | bytes 262144 | tf_op jit(solution)/shard_map/all_to_all | solution.py:90
  152.0 3.6 %gather_fusion.5 = bf16[128,4096]{1,0:T(8,128)(2,1)S(1)} fusion(bf16[128,4096]{1,0:T(8,128)(2,1)} %bitcast.15, s32[1024]{0:T(1024)S(1)} %pad_clamp_fusion), kind=kCustom, calls=%fused_computation.5 | custom fusion | bytes 2097664 | tf_op jit(solution)/shard_map/gather | solution.py:81
  155.8 85.8 %while.25 = (s32[]{:T(128)}, f32[8,16,256]{2,1,0:T(8,128)S(1)}, bf16[8,16,4096]{2,1,0:T(8,128)(2,1)S(1)}, bf16[8,16,4352]{2,1,0:T(8,128)(2,1)S(1)}, s32[]{:T(128)}, /*index=5*/f32[]{:T(128)}) while((s32[]{:T(128)}, f32[8,16,256]{2,1,0:T(8,128)S(1)}, bf16[8,16,4096]{2,1,0:T(8,128)(2,1)S(1)}, bf16[8,16,4352]{2,1,0:T(8,128)(2,1)S(1)}, s32[]{:T(128)}, ...), condition=%wide.region_7.8_spmd, body=%wide.region_5.7_spmd.sunk | while | flops 52293616 | bytes 45015304 | solution.py:43
  158.7 4.6 %reshape.415 = f32[16,128,385]{2,1,0:T(8,128)} reshape(f32[16,49280]{1,0:T(8,128)S(1)} %pad.76) | data formatting | bytes 6307840 | tf_op jit(solution)/shard_map/while/body/eval_jaxpr/reshape | solution.py:33
  169.4 4.6 %reshape.415 = f32[16,128,385]{2,1,0:T(8,128)} reshape(f32[16,49280]{1,0:T(8,128)S(1)} %pad.76) | data formatting | bytes 6307840 | tf_op jit(solution)/shard_map/while/body/eval_jaxpr/reshape | solution.py:33
  180.2 4.6 %reshape.415 = f32[16,128,385]{2,1,0:T(8,128)} reshape(f32[16,49280]{1,0:T(8,128)S(1)} %pad.76) | data formatting | bytes 6307840 | tf_op jit(solution)/shard_map/while/body/eval_jaxpr/reshape | solution.py:33
  190.9 4.6 %reshape.415 = f32[16,128,385]{2,1,0:T(8,128)} reshape(f32[16,49280]{1,0:T(8,128)S(1)} %pad.76) | data formatting | bytes 6307840 | tf_op jit(solution)/shard_map/while/body/eval_jaxpr/reshape | solution.py:33
  201.6 4.6 %reshape.415 = f32[16,128,385]{2,1,0:T(8,128)} reshape(f32[16,49280]{1,0:T(8,128)S(1)} %pad.76) | data formatting | bytes 6307840 | tf_op jit(solution)/shard_map/while/body/eval_jaxpr/reshape | solution.py:33
  212.3 4.6 %reshape.415 = f32[16,128,385]{2,1,0:T(8,128)} reshape(f32[16,49280]{1,0:T(8,128)S(1)} %pad.76) | data formatting | bytes 6307840 | tf_op jit(solution)/shard_map/while/body/eval_jaxpr/reshape | solution.py:33
  223.0 4.6 %reshape.415 = f32[16,128,385]{2,1,0:T(8,128)} reshape(f32[16,49280]{1,0:T(8,128)S(1)} %pad.76) | data formatting | bytes 6307840 | tf_op jit(solution)/shard_map/while/body/eval_jaxpr/reshape | solution.py:33
  233.8 4.6 %reshape.415 = f32[16,128,385]{2,1,0:T(8,128)} reshape(f32[16,49280]{1,0:T(8,128)S(1)} %pad.76) | data formatting | bytes 6307840 | tf_op jit(solution)/shard_map/while/body/eval_jaxpr/reshape | solution.py:33
  245.2 42.4 %all-reduce.5.cloned.1.call-done = f32[2,256,128]{2,0,1:T(2,128)} async-done(((f32[2,256,128]{2,0,1:T(2,128)}), f32[2,256,128]{2,0,1:T(2,128)}) %all-reduce.5.cloned.1.call-update) | async-done | bytes 262160
  (361 shorter events, 102.1 us)
Async XLA Ops:
  6.5 9.5 %copy-start = (bf16[16,4096]{1,0:T(8,128)(2,1)S(1)}, bf16[16,4096]{1,0:T(8,128)(2,1)}, u32[]{:S(2)}) copy-start(bf16[16,4096]{1,0:T(8,128)(2,1)} %param.8) | copy-start | bytes 393220
  9.7 11.8 %all-to-all-start.1 = ((s32[8,1,16]{2,1,0:T(1,128)}), s32[8,1,16]{2,1,0:T(1,128)S(1)}, u32[]{:S(2)}, u32[]{:S(2)}) async-start(s32[8,1,16]{2,1,0:T(1,128)} %bitcast.6), calls=%async_computation.1 | async-start | bytes 8192 | tf_op jit(solution)/shard_map/all_to_all | solution.py:74
  16.0 9.0 %copy-start.9 = (s32[16,4096]{1,0:T(8,128)S(1)}, s32[16,4096]{1,0:T(8,128)}, u32[]{:S(2)}) copy-start(s32[16,4096]{1,0:T(8,128)} %param.9) | copy-start | bytes 786436
  16.0 12.6 %copy-start.10 = (s32[16]{0:T(128)S(1)}, s32[16]{0:T(128)}, u32[]{:S(2)}) copy-start(s32[16]{0:T(128)} %param.11) | copy-start | bytes 196
  21.5 30.1 %all-to-all-start = ((bf16[8,16,4096]{2,1,0:T(8,128)(2,1)}), bf16[8,16,4096]{2,1,0:T(8,128)(2,1)S(1)}, u32[]{:S(2)}, u32[]{:S(2)}) async-start(bf16[8,16,4096]{2,1,0:T(8,128)(2,1)} %bitcast.4), calls=%async_computation | async-start | bytes 2097152 | tf_op jit(solution)/shard_map/all_to_all | solution.py:73
  25.1 7.3 %collective-permute-start = (bf16[16,256]{1,0:T(8,128)(2,1)S(1)}, bf16[16,256]{1,0:T(8,128)(2,1)S(1)}, u32[]{:S(2)}, u32[]{:S(2)}) collective-permute-start(bf16[16,256]{1,0:T(8,128)(2,1)S(1)} %slice.72), channel_id=1, source_target_pairs={{0,1},{1,2},{2,3},{4,5},{5,6},{6,7},{8,9},{9,10},{10,11},{12,13},{... | collective-permute-start | bytes 24584 | tf_op jit(solution)/shard_map/ppermute | solution.py:17
  51.6 95.2 %all-to-all-start.3 = ((bf16[8,16,4096]{2,1,0:T(8,128)(2,1)}), bf16[8,16,4096]{2,1,0:T(8,128)(2,1)}, u32[]{:S(2)}, u32[]{:S(2)}) async-start(bf16[8,16,4096]{2,1,0:T(8,128)(2,1)} %bitcast.14), calls=%async_computation.3 | async-start | bytes 2097152 | tf_op jit(solution)/shard_map/all_to_all | solution.py:79
  64.0 3.7 %copy-start.2 = (bf16[8,16,4352]{2,1,0:T(8,128)(2,1)S(1)}, bf16[8,16,4352]{2,1,0:T(8,128)(2,1)}, u32[]{:S(2)}) copy-start(bf16[8,16,4352]{2,1,0:T(8,128)(2,1)} %copy-done.1) | copy-start | bytes 3342340 | tf_op jit(solution)/shard_map/while
  64.0 3.7 %copy-start.8 = (bf16[8,16,4096]{2,1,0:T(8,128)(2,1)S(1)}, bf16[8,16,4096]{2,1,0:T(8,128)(2,1)}, u32[]{:S(2)}) copy-start(bf16[8,16,4096]{2,1,0:T(8,128)(2,1)} %copy-done.7) | copy-start | bytes 3145732 | tf_op jit(solution)/shard_map/while
  75.3 3.7 %copy-start.2 = (bf16[8,16,4352]{2,1,0:T(8,128)(2,1)S(1)}, bf16[8,16,4352]{2,1,0:T(8,128)(2,1)}, u32[]{:S(2)}) copy-start(bf16[8,16,4352]{2,1,0:T(8,128)(2,1)} %copy-done.1) | copy-start | bytes 3342340 | tf_op jit(solution)/shard_map/while
  75.3 3.7 %copy-start.8 = (bf16[8,16,4096]{2,1,0:T(8,128)(2,1)S(1)}, bf16[8,16,4096]{2,1,0:T(8,128)(2,1)}, u32[]{:S(2)}) copy-start(bf16[8,16,4096]{2,1,0:T(8,128)(2,1)} %copy-done.7) | copy-start | bytes 3145732 | tf_op jit(solution)/shard_map/while
  86.6 3.7 %copy-start.2 = (bf16[8,16,4352]{2,1,0:T(8,128)(2,1)S(1)}, bf16[8,16,4352]{2,1,0:T(8,128)(2,1)}, u32[]{:S(2)}) copy-start(bf16[8,16,4352]{2,1,0:T(8,128)(2,1)} %copy-done.1) | copy-start | bytes 3342340 | tf_op jit(solution)/shard_map/while
  86.6 3.7 %copy-start.8 = (bf16[8,16,4096]{2,1,0:T(8,128)(2,1)S(1)}, bf16[8,16,4096]{2,1,0:T(8,128)(2,1)}, u32[]{:S(2)}) copy-start(bf16[8,16,4096]{2,1,0:T(8,128)(2,1)} %copy-done.7) | copy-start | bytes 3145732 | tf_op jit(solution)/shard_map/while
  97.9 3.7 %copy-start.2 = (bf16[8,16,4352]{2,1,0:T(8,128)(2,1)S(1)}, bf16[8,16,4352]{2,1,0:T(8,128)(2,1)}, u32[]{:S(2)}) copy-start(bf16[8,16,4352]{2,1,0:T(8,128)(2,1)} %copy-done.1) | copy-start | bytes 3342340 | tf_op jit(solution)/shard_map/while
  97.9 3.7 %copy-start.8 = (bf16[8,16,4096]{2,1,0:T(8,128)(2,1)S(1)}, bf16[8,16,4096]{2,1,0:T(8,128)(2,1)}, u32[]{:S(2)}) copy-start(bf16[8,16,4096]{2,1,0:T(8,128)(2,1)} %copy-done.7) | copy-start | bytes 3145732 | tf_op jit(solution)/shard_map/while
  109.2 3.7 %copy-start.2 = (bf16[8,16,4352]{2,1,0:T(8,128)(2,1)S(1)}, bf16[8,16,4352]{2,1,0:T(8,128)(2,1)}, u32[]{:S(2)}) copy-start(bf16[8,16,4352]{2,1,0:T(8,128)(2,1)} %copy-done.1) | copy-start | bytes 3342340 | tf_op jit(solution)/shard_map/while
  109.2 3.7 %copy-start.8 = (bf16[8,16,4096]{2,1,0:T(8,128)(2,1)S(1)}, bf16[8,16,4096]{2,1,0:T(8,128)(2,1)}, u32[]{:S(2)}) copy-start(bf16[8,16,4096]{2,1,0:T(8,128)(2,1)} %copy-done.7) | copy-start | bytes 3145732 | tf_op jit(solution)/shard_map/while
  120.5 3.7 %copy-start.2 = (bf16[8,16,4352]{2,1,0:T(8,128)(2,1)S(1)}, bf16[8,16,4352]{2,1,0:T(8,128)(2,1)}, u32[]{:S(2)}) copy-start(bf16[8,16,4352]{2,1,0:T(8,128)(2,1)} %copy-done.1) | copy-start | bytes 3342340 | tf_op jit(solution)/shard_map/while
  120.5 3.7 %copy-start.8 = (bf16[8,16,4096]{2,1,0:T(8,128)(2,1)S(1)}, bf16[8,16,4096]{2,1,0:T(8,128)(2,1)}, u32[]{:S(2)}) copy-start(bf16[8,16,4096]{2,1,0:T(8,128)(2,1)} %copy-done.7) | copy-start | bytes 3145732 | tf_op jit(solution)/shard_map/while
  131.8 3.7 %copy-start.2 = (bf16[8,16,4352]{2,1,0:T(8,128)(2,1)S(1)}, bf16[8,16,4352]{2,1,0:T(8,128)(2,1)}, u32[]{:S(2)}) copy-start(bf16[8,16,4352]{2,1,0:T(8,128)(2,1)} %copy-done.1) | copy-start | bytes 3342340 | tf_op jit(solution)/shard_map/while
  131.8 3.7 %copy-start.8 = (bf16[8,16,4096]{2,1,0:T(8,128)(2,1)S(1)}, bf16[8,16,4096]{2,1,0:T(8,128)(2,1)}, u32[]{:S(2)}) copy-start(bf16[8,16,4096]{2,1,0:T(8,128)(2,1)} %copy-done.7) | copy-start | bytes 3145732 | tf_op jit(solution)/shard_map/while
  143.1 3.7 %copy-start.2 = (bf16[8,16,4352]{2,1,0:T(8,128)(2,1)S(1)}, bf16[8,16,4352]{2,1,0:T(8,128)(2,1)}, u32[]{:S(2)}) copy-start(bf16[8,16,4352]{2,1,0:T(8,128)(2,1)} %copy-done.1) | copy-start | bytes 3342340 | tf_op jit(solution)/shard_map/while
  143.1 3.7 %copy-start.8 = (bf16[8,16,4096]{2,1,0:T(8,128)(2,1)S(1)}, bf16[8,16,4096]{2,1,0:T(8,128)(2,1)}, u32[]{:S(2)}) copy-start(bf16[8,16,4096]{2,1,0:T(8,128)(2,1)} %copy-done.7) | copy-start | bytes 3145732 | tf_op jit(solution)/shard_map/while
  146.8 94.7 %all-to-all-start.2 = ((f32[8,16,256]{2,1,0:T(8,128)}), f32[8,16,256]{2,1,0:T(8,128)S(1)}, u32[]{:S(2)}, u32[]{:S(2)}) async-start(f32[8,16,256]{2,1,0:T(8,128)} %get-tuple-element.111), calls=%async_computation.2 | async-start | bytes 262144 | tf_op jit(solution)/shard_map/all_to_all | solution.py:90
  151.8 135.8 %all-reduce.5.cloned.1.call-start = ((), (), s32[]{:S(2)}) async-start(), calls=%async_computation.4 | async-start | bytes 524288
  163.3 3.1 %copy-start.6 = (bf16[8,16,4096]{2,1,0:T(8,128)(2,1)S(1)}, bf16[8,16,4096]{2,1,0:T(8,128)(2,1)}, u32[]{:S(2)}) copy-start(bf16[8,16,4096]{2,1,0:T(8,128)(2,1)} %copy-done.5) | copy-start | bytes 3145732 | tf_op jit(solution)/shard_map/while
  174.0 3.1 %copy-start.6 = (bf16[8,16,4096]{2,1,0:T(8,128)(2,1)S(1)}, bf16[8,16,4096]{2,1,0:T(8,128)(2,1)}, u32[]{:S(2)}) copy-start(bf16[8,16,4096]{2,1,0:T(8,128)(2,1)} %copy-done.5) | copy-start | bytes 3145732 | tf_op jit(solution)/shard_map/while
  184.8 3.1 %copy-start.6 = (bf16[8,16,4096]{2,1,0:T(8,128)(2,1)S(1)}, bf16[8,16,4096]{2,1,0:T(8,128)(2,1)}, u32[]{:S(2)}) copy-start(bf16[8,16,4096]{2,1,0:T(8,128)(2,1)} %copy-done.5) | copy-start | bytes 3145732 | tf_op jit(solution)/shard_map/while
  195.5 3.1 %copy-start.6 = (bf16[8,16,4096]{2,1,0:T(8,128)(2,1)S(1)}, bf16[8,16,4096]{2,1,0:T(8,128)(2,1)}, u32[]{:S(2)}) copy-start(bf16[8,16,4096]{2,1,0:T(8,128)(2,1)} %copy-done.5) | copy-start | bytes 3145732 | tf_op jit(solution)/shard_map/while
  206.2 3.1 %copy-start.6 = (bf16[8,16,4096]{2,1,0:T(8,128)(2,1)S(1)}, bf16[8,16,4096]{2,1,0:T(8,128)(2,1)}, u32[]{:S(2)}) copy-start(bf16[8,16,4096]{2,1,0:T(8,128)(2,1)} %copy-done.5) | copy-start | bytes 3145732 | tf_op jit(solution)/shard_map/while
  216.9 3.1 %copy-start.6 = (bf16[8,16,4096]{2,1,0:T(8,128)(2,1)S(1)}, bf16[8,16,4096]{2,1,0:T(8,128)(2,1)}, u32[]{:S(2)}) copy-start(bf16[8,16,4096]{2,1,0:T(8,128)(2,1)} %copy-done.5) | copy-start | bytes 3145732 | tf_op jit(solution)/shard_map/while
  227.6 3.1 %copy-start.6 = (bf16[8,16,4096]{2,1,0:T(8,128)(2,1)S(1)}, bf16[8,16,4096]{2,1,0:T(8,128)(2,1)}, u32[]{:S(2)}) copy-start(bf16[8,16,4096]{2,1,0:T(8,128)(2,1)} %copy-done.5) | copy-start | bytes 3145732 | tf_op jit(solution)/shard_map/while
  (41 other events, 115.2 us)
Sparse Core Ops, SparseCore 0:
  243.4 44.1 all-reduce.4
where the time goes:
time: 296 us
  local copies, waits for them, and re-layouts  135 us (46%)
  waiting for transfers between devices  63.6 us (21%)
  other arithmetic  48.4 us (16%)
  starting transfers between devices  22.8 us (8%)
  between operations  14.3 us (5%)
  matrix products  9.84 us (3%)
    reshape x16, local copies, waits for them, and re-layouts, correlate_group(): skewed = spread.reshape(count, BLOCK, width + 1)  73.7 us
    reduce_sum x16, other arithmetic, correlate_group(): totals = jnp.sum(skewed, axis=1)  46.5 us
    unnamed x2, waiting for transfers between devices  42.5 us
    while x176, local copies, waits for them, and re-layouts  30 us
    all_to_all x1, waiting for transfers between devices, per_device(): lax.all_to_all(send_rows, 'lane', split_axis=0, concat_axis=0, tiled=True)  17.8 us
    dot_general x16, matrix products, correlate_group(): jnp.einsum('rbi,rbj->rij', row_blocks, window, preferred_element_type=jnp...  9.84 us
    all_to_all x1, starting transfers between devices, per_device(): lax.all_to_all(send_index, 'lane', split_axis=0, concat_axis=0, tiled=True)  6.33 us
  transfers between devices with their start and end apart: 6, of which 3 were waited for; matrix products, arithmetic and copies ran while one was open for 63% of the time, Pallas kernels for 0%

commit v1 on v0

v1 whole, which is shorter than its diff:
```python
import functools

import jax
import jax.numpy as jnp
from jax import lax
from jax.experimental import pallas as pl
from jax.experimental.pallas import tpu as pltpu
from jax.sharding import PartitionSpec as P

LAGS = 256
FINE = 16
STEPS = LAGS // FINE
MESH = pl.DeviceIdType.MESH
F32 = jnp.float32
BF16 = jnp.bfloat16


def nn(a, b):
    return lax.dot_general(a, b, (((1,), (0,)), ((), ())), preferred_element_type=F32)


def nt(a, b):
    return lax.dot_general(a, b, (((1,), (1,)), ((), ())), preferred_element_type=F32)


def pieces(x, count):
    parts = []
    for _ in range(count):
        part = x.astype(BF16)
        parts.append(part)
        x = x - part.astype(F32)
    return parts


def iota(shape, axis):
    return lax.broadcasted_iota(jnp.int32, shape, axis)


def kernel(
    n_lane, n_rec, slots, scale, chunks,
    w_ref, pat_ref, meta_ref, out_ref,
    wall, metas, rim, halo, shifted, refs, acc, zbuf, zin, fout, fin,
    send_d, recv_d, send_s, recv_s, send_m, recv_m, send_h, recv_h,
    send_z, recv_z, send_f, recv_f,
):
    lane_dev, time_dev = w_ref.shape
    lanes = lane_dev * n_lane
    pairs = lane_dev * slots
    n_z = n_lane // 2
    lag_dev = LAGS // n_rec
    per_rec = STEPS // n_rec
    cols = FINE * lane_dev
    wide = time_dev // chunks
    me = lax.axis_index("lane")
    rec = lax.axis_index("rec")
    z, core = me // 2, me % 2
    sibling = 2 * z + 1 - core

    barrier = pltpu.get_barrier_semaphore()
    for off in range(1, n_lane):
        pl.semaphore_signal(
            barrier, inc=1, device_id={"lane": (me + off) % n_lane}, device_id_type=MESH
        )
    for off in range(1, n_rec):
        pl.semaphore_signal(
            barrier, inc=1, device_id={"rec": (rec + off) % n_rec}, device_id_type=MESH
        )

    def rows_of(owner):
        return pl.ds(pl.multiple_of(owner * lane_dev, lane_dev), lane_dev)

    def remote(src, dst, send, recv, where):
        return pltpu.make_async_remote_copy(
            src_ref=src, dst_ref=dst, send_sem=send, recv_sem=recv,
            device_id=where, device_id_type=MESH,
        )

    levels = (2 * pat_ref[...] - 3).astype(F32)
    rim[...] = levels[:, time_dev - LAGS :].astype(BF16)
    metas[rows_of(me), :] = meta_ref[...]
    wall[rows_of(me), :] = w_ref[...]

    pl.semaphore_wait(barrier, n_lane - 1 + n_rec - 1)

    sent = []
    to_next = remote(rim, halo, send_h.at[0], recv_h.at[0], {"rec": (rec + 1) % n_rec})
    to_next.start()
    sent.append(to_next)

    def span(c):
        return pl.ds(c * wide, wide)

    def direct(off, c):
        return remote(
            w_ref.at[:, span(c)], wall.at[rows_of(me), span(c)],
            send_d.at[off, c], recv_d.at[off, c],
            {"lane": 2 * ((z + off) % n_z) + core},
        )

    def arrived(off, c):
        block = wall.at[rows_of(2 * ((z + n_z - off) % n_z) + core), span(c)]
        return remote(block, block, send_d.at[off, c], recv_d.at[off, c], {"lane": sibling})

    def across(off, c):
        block = wall.at[rows_of(2 * ((z + n_z - off) % n_z) + core), span(c)]
        return remote(block, block, send_s.at[off, c], recv_s.at[off, c], {"lane": sibling})

    def crossed(off, c):
        block = wall.at[rows_of(2 * ((z + n_z - off) % n_z) + 1 - core), span(c)]
        return remote(block, block, send_s.at[off, c], recv_s.at[off, c], {"lane": sibling})

    for c in range(chunks):
        for off in range(1, n_z):
            copy = direct(off, c)
            copy.start()
            sent.append(copy)
        copy = across(0, c)
        copy.start()
        sent.append(copy)
    for off in range(1, n_lane):
        copy = remote(
            meta_ref, metas.at[rows_of(me), :], send_m.at[off], recv_m.at[off],
            {"lane": (me + off) % n_lane},
        )
        copy.start()
        sent.append(copy)

    to_next.wait_recv()
    before = jnp.where(rec > 0, halo[...].astype(F32), 0.0)
    extended = jnp.concatenate([before, levels], axis=1)
    for r in range(FINE):
        moved = extended if r == 0 else pltpu.roll(extended, r, 1)
        shifted[r * lane_dev : (r + 1) * lane_dev, :] = moved.astype(BF16)
    unit = (iota((LAGS, LAGS), 0) == iota((LAGS, LAGS), 1)).astype(BF16)
    for b in range((time_dev + LAGS) // LAGS):
        part = slice(b * LAGS, (b + 1) * LAGS)
        refs[part, :] = nt(unit, shifted[:, part]).astype(BF16)

    def multiply(c):
        group = 4

        def body(step, carry):
            for i in range(group):
                a = step * group + i
                start = pl.multiple_of(c * wide + LAGS - FINE * a, FINE)
                term = nn(wall[:, c * wide : (c + 1) * wide], refs[pl.ds(start, wide), :])
                if c == 0:
                    acc[a] = term
                else:
                    acc[a] += term
            return carry

        lax.fori_loop(0, STEPS // group, body, 0)

    for c in range(chunks + 1):
        if c < chunks:
            for off in range(1, n_z):
                arrived(off, c).wait_recv()
                copy = across(off, c)
                copy.start()
                sent.append(copy)
        if c > 0:
            for off in range(n_z):
                crossed(off, c - 1).wait_recv()
            multiply(c - 1)

    for off in range(1, n_lane):
        owner = (me + n_lane - off) % n_lane
        block = metas.at[rows_of(owner), :]
        remote(block, block, send_m.at[off], recv_m.at[off], {"lane": sibling}).wait_recv()
    every = metas[...]
    inside = every - me * lane_dev
    mine = (inside >= 0) & (inside < lane_dev) & (iota(every.shape, 1) < slots)
    named = jnp.sum(jnp.where(mine, (inside + 1).astype(F32), 0.0), axis=1, keepdims=True) - 1.0
    column_lane = iota((lanes, cols), 1) % lane_dev
    keep_forward = named == column_lane.astype(F32)
    own = meta_ref[...]
    spread = (iota((pairs, lane_dev), 0) // slots == iota((pairs, lane_dev), 1)).astype(BF16)
    low, high = own % 64, own // 64
    tall = 64.0 * nn(spread, high.astype(F32).astype(BF16)) + nn(spread, low.astype(F32).astype(BF16))
    at_slot = iota(tall.shape, 1) == iota(tall.shape, 0) % slots
    target = jnp.sum(jnp.where(at_slot, tall, 0.0), axis=1, keepdims=True).astype(jnp.int32)
    pick = (target == iota((pairs, lanes), 1)).astype(BF16)
    keep_reverse = iota((pairs, cols), 1) % lane_dev == iota((pairs, cols), 0) // slots
    place = (
        (target // lane_dev) * lane_dev + iota((pairs, lanes), 0) // slots
        == iota((pairs, lanes), 1)
    ).astype(BF16)
    gather = (iota((FINE, cols), 1) // lane_dev == iota((FINE, cols), 0)).astype(BF16)
    pair_row = iota((lane_dev, pairs), 1)
    listed = (pair_row // slots == iota((lane_dev, pairs), 0)) & (
        pair_row % slots < own[:, slots : slots + 1]
    )
    gain = jnp.sum(jnp.where(listed, F32(scale), 0.0), axis=0, keepdims=True)

    for off in list(range(1, n_rec)) + [0]:
        there = (rec + off) % n_rec
        for i in range(per_rec):
            full = acc[there * per_rec + i]
            total_f = jnp.zeros((FINE, lanes), F32)
            total_r = jnp.zeros((FINE, pairs), F32)
            for part in pieces(full, 2):
                forward = jnp.where(keep_forward, part.astype(F32), 0.0).astype(BF16)
                total_f += nt(gather, forward)
                reverse = jnp.where(keep_reverse, nn(pick, part), 0.0).astype(BF16)
                total_r += nt(gather, reverse)
            zbuf[off, i * FINE : (i + 1) * FINE, 0:lanes] = total_f
            zbuf[off, i * FINE : (i + 1) * FINE, lanes : lanes + pairs] = total_r
        if off > 0:
            copy = remote(
                zbuf.at[off], zin.at[off], send_z.at[off], recv_z.at[off], {"rec": there}
            )
            copy.start()
            sent.append(copy)

    total = zbuf[0]
    for off in range(1, n_rec):
        remote(
            zbuf.at[off], zin.at[off], send_z.at[off], recv_z.at[off], {"lane": sibling}
        ).wait_recv()
        total += zin[off]

    line = (iota((lanes, lanes), 0) == iota((lanes, lanes), 1)).astype(BF16)
    forward_sum = total[:, 0:lanes]
    if lag_dev < 128:
        forward_sum = jnp.concatenate(
            [forward_sum, jnp.zeros((128 - lag_dev, lanes), F32)], axis=0
        )
    turned = jnp.zeros((lanes, 128), F32)
    for part in pieces(forward_sum, 3):
        turned += nt(line, part)
    fout[...] = turned
    fin[rows_of(me), :] = fout[rows_of(me), :]
    for off in range(1, n_lane):
        there = (me + off) % n_lane
        copy = remote(
            fout.at[rows_of(there), :], fin.at[rows_of(me), :],
            send_f.at[off], recv_f.at[off], {"lane": there},
        )
        copy.start()
        sent.append(copy)
    out_ref[1] = total[:, lanes : lanes + pairs] * gain
    for off in range(1, n_lane):
        block = fin.at[rows_of((me + n_lane - off) % n_lane), :]
        remote(block, block, send_f.at[off], recv_f.at[off], {"lane": sibling}).wait_recv()
    placed = jnp.zeros((pairs, 128), F32)
    for part in pieces(fin[...], 3):
        placed += nn(place, part)
    back = (iota((lag_dev, 128), 0) == iota((lag_dev, 128), 1)).astype(BF16)
    final = jnp.zeros((lag_dev, pairs), F32)
    for part in pieces(placed, 3):
        final += nt(back, part)
    out_ref[0] = final * gain
    for copy in sent:
        copy.wait_send()


def per_device(waveforms, patterns, partners, counts):
    lane_dev, time_dev = waveforms.shape
    slots = partners.shape[1]
    n_lane, n_rec = lax.axis_size("lane"), lax.axis_size("rec")
    lanes, pairs = lane_dev * n_lane, lane_dev * slots
    n_z = n_lane // 2
    lag_dev = LAGS // n_rec
    cols = FINE * lane_dev
    chunks = 4
    scale = (5.0 * time_dev * n_rec) ** -0.5
    meta = jnp.concatenate([partners, counts[:, None]], axis=1)
    meta = jnp.pad(meta, ((0, 0), (0, 128 - slots - 1)))
    dma = pltpu.SemaphoreType.DMA
    return pl.pallas_call(
        functools.partial(kernel, n_lane, n_rec, slots, scale, chunks),
        out_shape=jax.ShapeDtypeStruct((2, lag_dev, pairs), F32),
        in_specs=[pl.BlockSpec(memory_space=pltpu.VMEM)] * 3,
        out_specs=pl.BlockSpec(memory_space=pltpu.VMEM),
        scratch_shapes=[
            pltpu.VMEM((lanes, time_dev), BF16),
            pltpu.VMEM((lanes, 128), jnp.int32),
            pltpu.VMEM((lane_dev, LAGS), BF16),
            pltpu.VMEM((lane_dev, LAGS), BF16),
            pltpu.VMEM((cols, time_dev + LAGS), BF16),
            pltpu.VMEM((time_dev + LAGS, cols), BF16),
            pltpu.VMEM((STEPS, lanes, cols), F32),
            pltpu.VMEM((n_rec, lag_dev, lanes + pairs), F32),
            pltpu.VMEM((n_rec, lag_dev, lanes + pairs), F32),
            pltpu.VMEM((lanes, 128), F32),
            pltpu.VMEM((lanes, 128), F32),
            dma((n_z, chunks)), dma((n_z, chunks)),
            dma((n_z, chunks)), dma((n_z, chunks)),
            dma((n_lane,)), dma((n_lane,)),
            dma((1,)), dma((1,)),
            dma((n_rec,)), dma((n_rec,)),
            dma((n_lane,)), dma((n_lane,)),
        ],
        compiler_params=pltpu.CompilerParams(
            collective_id=0, has_side_effects=True, vmem_limit_bytes=48 * 1024 * 1024
        ),
    )(waveforms, patterns, meta)


def solution(mesh):
    in_specs = (P("lane", "rec"), P("lane", "rec"), P("lane", None), P("lane"))
    out_specs = P(None, "rec", "lane")
    return jax.shard_map(
        per_device, mesh=mesh, in_specs=in_specs, out_specs=out_specs, check_vma=False
    )
```

time: 296 us -> 39.4 us (0.13)
  local copies, waits for them, and re-layouts: 135 us -> 3.35 us
  waiting for transfers between devices: 63.6 us -> 0 us
  other arithmetic: 48.4 us -> 0.08 us
  Pallas kernels: 0 us -> 35.8 us
  starting transfers between devices: 22.8 us -> 0 us
  between operations: 14.3 us -> 0.01 us
  matrix products: 9.84 us -> 0 us
    reshape x35 -> x0, local copies, waits for them, and re-layouts: 75.2 us -> none  [the longest x16 73.7 us: correlate_group(): skewed = spread.reshape(count, BLOCK, width + 1)]
    reduce_sum x18 -> x0, other arithmetic: 46.8 us -> none  [the longest x16 46.5 us: correlate_group(): totals = jnp.sum(skewed, axis=1)]
    unnamed x2 -> x0, waiting for transfers between devices: 42.5 us -> none
    pallas_call x0 -> x1, Pallas kernels: none -> 35.8 us  [per_device(): pl.pallas_call(functools.partial(kernel, n_lane, n_rec, slots, scale, chu...]
    while x176 -> x0, local copies, waits for them, and re-layouts: 30 us -> none
    all_to_all x4 -> x0, waiting for transfers between devices: 21.1 us -> none  [the longest x1 17.8 us: per_device(): lax.all_to_all(send_rows, 'lane', split_axis=0, concat_axis=0, tiled=True)]
    all_to_all x4 -> x0, starting transfers between devices: 19.1 us -> none  [the longest x1 6.33 us: per_device(): lax.all_to_all(send_index, 'lane', split_axis=0, concat_axis=0, tiled=True)]
    gather x6 -> x0, local copies, waits for them, and re-layouts: 11.2 us -> none  [the longest x1 3.56 us: per_device(): reverse_rows = returned.reshape(lane_count * capacity, time_dev)[slot_of]]
  transfers between devices with their start and end apart: 6 -> 0, of which waited for: 3 -> 0; matrix products, arithmetic and copies ran while one was open for 63% -> 0% of each run, Pallas kernels for 0% -> 0%
where the time goes in v1:
time: 39.4 us; the launch traced here: 39.2 us
  Pallas kernels  35.8 us (91%)
  local copies, waits for them, and re-layouts  3.35 us (9%)
    pallas_call x1, Pallas kernels, per_device(): pl.pallas_call(functools.partial(kernel, n_lane, n_rec, slots, scale, chu...  35.8 us
    unnamed x8, local copies, waits for them, and re-layouts  3.26 us

profile of v1, /device:TPU:0, one launch (start us, length us, event | category | flops | bytes accessed | tf_op | source)
XLA Modules:
  0.0 39.2 jit_solution(1064297525940721800)
XLA Ops:
  0.0 0.0 copy-start.2
  0.0 0.8 %copy.5 = s32[16,8]{1,0:T(8,128)S(1)} copy(s32[16,8]{0,1:T(8,128)} %param.6) | data formatting | bytes 1024 | tf_op args[2]
  0.8 0.0 copy-done.2
  0.8 0.1 copy.6
  0.9 0.1 pad_add_fusion
  0.9 0.0 copy-start
  0.9 0.9 %copy-done = s32[16,4096]{1,0:T(8,128)S(1)} copy-done((s32[16,4096]{1,0:T(8,128)S(1)}, s32[16,4096]{1,0:T(8,128)}, u32[]{:S(2)}) %copy-start) | copy-done | bytes 262168
  1.9 0.0 copy-start.1
  1.9 0.9 %copy-done.1 = bf16[16,4096]{1,0:T(8,128)(2,1)S(1)} copy-done((bf16[16,4096]{1,0:T(8,128)(2,1)S(1)}, bf16[16,4096]{1,0:T(8,128)(2,1)}, u32[]{:S(2)}) %copy-start.1) | copy-done | bytes 131096
  2.8 35.8 %shard_map.46 = f32[2,64,128]{2,1,0:T(8,128)S(1)} custom-call(bf16[16,4096]{1,0:T(8,128)(2,1)S(1)} %copy-done.1, s32[16,4096]{1,0:T(8,128)S(1)} %copy-done, s32[16,128]{1,0:T(8,128)S(1)} %pad.4.meta_ref), custom_call_target="tpu_custom_call" | custom-call | tf_op jit(solution)/shard_map/pallas_call | solution.py:271
  38.6 0.6 %copy.8 = f32[2,64,128]{2,1,0:T(8,128)} copy(f32[2,64,128]{2,1,0:T(8,128)S(1)} %shard_map.46) | data formatting | bytes 131072
  (1 shorter events, 0.0 us)
Async XLA Ops:
  0.0 0.8 %copy-start.2 = (s32[16]{0:T(128)S(1)}, s32[16]{0:T(128)}, u32[]{:S(2)}) copy-start(s32[16]{0:T(128)} %param.7) | copy-start | bytes 196
  0.9 1.0 %copy-start = (s32[16,4096]{1,0:T(8,128)S(1)}, s32[16,4096]{1,0:T(8,128)}, u32[]{:S(2)}) copy-start(s32[16,4096]{1,0:T(8,128)} %pat_ref.1) | copy-start | bytes 786436
  1.9 0.9 %copy-start.1 = (bf16[16,4096]{1,0:T(8,128)(2,1)S(1)}, bf16[16,4096]{1,0:T(8,128)(2,1)}, u32[]{:S(2)}) copy-start(bf16[16,4096]{1,0:T(8,128)(2,1)} %w_ref.1) | copy-start | bytes 393220

commit v2 on v1

v2 whole, which is shorter than its diff:
```python
import functools

import jax
import jax.numpy as jnp
from jax import lax
from jax.experimental import pallas as pl
from jax.experimental.pallas import tpu as pltpu
from jax.sharding import PartitionSpec as P

LAGS = 256
HALF = 128
MESH = pl.DeviceIdType.MESH
F32 = jnp.float32
BF16 = jnp.bfloat16


def nn(a, b):
    return lax.dot_general(a, b, (((1,), (0,)), ((), ())), preferred_element_type=F32)


def nt(a, b):
    return lax.dot_general(a, b, (((1,), (1,)), ((), ())), preferred_element_type=F32)


def pieces(x, count):
    parts = []
    for _ in range(count):
        part = x.astype(BF16)
        parts.append(part)
        x = x - part.astype(F32)
    return parts


def iota(shape, axis):
    return lax.broadcasted_iota(jnp.int32, shape, axis)


def spread_out(values, where):
    low, high = values % 64, values // 64
    low, high = low.astype(F32).astype(BF16), high.astype(F32).astype(BF16)
    return 64.0 * nn(high, where) + nn(low, where)


def kernel(
    n_lane, n_rec, scale, chunks,
    w_ref, pat_ref, partners_ref, counts_ref, out_ref,
    wall, pats, ext, named, rim, halo, delayed, acc, zbuf, zin, fout, fin,
    local_w, local_p, send_d, recv_d, send_s, recv_s, send_m, recv_m, send_h, recv_h,
    send_z, recv_z, send_f, recv_f,
):
    lane_dev, time_dev = w_ref.shape
    slots = partners_ref.shape[0]
    lanes = lane_dev * n_lane
    pairs = lane_dev * slots
    n_z = n_lane // 2
    lag_dev = LAGS // n_rec
    wide = time_dev // chunks
    me = lax.axis_index("lane")
    rec = lax.axis_index("rec")
    z, core = me // 2, me % 2
    sibling = 2 * z + 1 - core

    barrier = pltpu.get_barrier_semaphore()
    for off in range(1, n_lane):
        pl.semaphore_signal(
            barrier, inc=1, device_id={"lane": (me + off) % n_lane}, device_id_type=MESH
        )
    for off in range(1, n_rec):
        pl.semaphore_signal(
            barrier, inc=1, device_id={"rec": (rec + off) % n_rec}, device_id_type=MESH
        )

    def rows_of(owner):
        return pl.ds(pl.multiple_of(owner * lane_dev, lane_dev), lane_dev)

    def remote(src, dst, send, recv, where):
        return pltpu.make_async_remote_copy(
            src_ref=src, dst_ref=dst, send_sem=send, recv_sem=recv,
            device_id=where, device_id_type=MESH,
        )

    def span(c):
        return pl.ds(HALF + c * wide, wide)

    def from_chip(off, same):
        return rows_of(2 * ((z + n_z - off) % n_z) + (core if same else 1 - core))

    take_p = pltpu.make_async_copy(pat_ref, pats, local_p.at[0])
    take_p.start()
    take_w = pltpu.make_async_copy(
        w_ref, wall.at[rows_of(me), pl.ds(HALF, time_dev)], local_w.at[0]
    )
    take_w.start()
    edge = jnp.zeros((lanes, HALF), BF16)
    wall[:, 0:HALF] = edge
    wall[:, HALF + time_dev : 2 * HALF + time_dev] = edge
    spot = (iota((lane_dev, lanes), 0) + me * lane_dev == iota((lane_dev, lanes), 1)).astype(BF16)
    inside = spread_out(partners_ref[...] + 1, spot)
    named[0] = inside
    take_p.wait()
    levels = (2 * pats[...] - 3).astype(F32)
    ext[:, LAGS : LAGS + time_dev] = levels
    rim[...] = levels[:, time_dev - LAGS :].astype(BF16)

    pl.semaphore_wait(barrier, n_lane - 1 + n_rec - 1)

    sent = []

    def go(copy):
        copy.start()
        sent.append(copy)

    to_next = remote(rim, halo, send_h.at[0], recv_h.at[0], {"rec": (rec + 1) % n_rec})
    go(to_next)
    for c in range(chunks):
        part = w_ref.at[:, pl.ds(c * wide, wide)]
        for off in range(1, n_z):
            go(
                remote(
                    part, wall.at[rows_of(me), span(c)], send_d.at[off, c], recv_d.at[off, c],
                    {"lane": 2 * ((z + off) % n_z) + core},
                )
            )
        go(
            remote(
                part, wall.at[rows_of(me), span(c)], send_s.at[0, c], recv_s.at[0, c],
                {"lane": sibling},
            )
        )
    for off in range(1, n_lane):
        go(
            remote(
                named.at[0], named.at[off], send_m.at[off], recv_m.at[off],
                {"lane": (me + off) % n_lane},
            )
        )

    to_next.wait_recv()
    ext[:, 0:LAGS] = jnp.where(rec > 0, halo[...].astype(F32), 0.0)

    def width_of(c):
        return wide + (HALF if c == chunks - 1 else 0)

    def delay(c):
        def body(m, carry):
            row = ext[pl.ds(m, 1), c * wide : c * wide + width_of(c) + HALF]
            same = jnp.broadcast_to(row, (HALF, width_of(c) + HALF))
            moved = pltpu.roll(same, 0, 1, stride=1, stride_axis=0)
            delayed[pl.ds(pl.multiple_of(m * HALF, HALF), HALF), c * wide : c * wide + width_of(c)] = (
                moved[:, HALF:].astype(BF16)
            )
            return carry

        lax.fori_loop(0, lane_dev, body, 0)

    group = 4

    def multiply(c):
        def body(g, carry):
            first = wall[:, c * wide : c * wide + width_of(c)]
            second = wall[:, c * wide + HALF : c * wide + width_of(c) + HALF]
            held = jnp.concatenate([first, second], axis=0)
            rows = pl.ds(pl.multiple_of(g * group * HALF, group * HALF), group * HALF)
            term = nt(delayed[rows, c * wide : c * wide + width_of(c)], held)
            if c == 0:
                acc[rows, :] = term
            else:
                acc[rows, :] += term
            return carry

        lax.fori_loop(0, lane_dev // group, body, 0)

    for c in range(chunks + 1):
        if c < chunks:
            delay(c)
            for off in range(1, n_z):
                block = wall.at[from_chip(off, True), span(c)]
                remote(
                    block, block, send_d.at[off, c], recv_d.at[off, c], {"lane": sibling}
                ).wait_recv()
                go(remote(block, block, send_s.at[off, c], recv_s.at[off, c], {"lane": sibling}))
        if c == 1:
            take_w.wait()
        if c > 0:
            for off in range(n_z):
                block = wall.at[from_chip(off, False), span(c - 1)]
                remote(
                    block, block, send_s.at[off, c - 1], recv_s.at[off, c - 1], {"lane": sibling}
                ).wait_recv()
            multiply(c - 1)

    for off in range(1, n_lane):
        remote(
            named.at[off], named.at[off], send_m.at[off], recv_m.at[off], {"lane": sibling}
        ).wait_recv()
        inside = inside + named[off]
    local = inside - 1.0 - (me * lane_dev).astype(F32)
    here = (local >= 0.0) & (local < float(lane_dev))
    mine = jnp.sum(jnp.where(here, local + 1.0, 0.0), axis=0, keepdims=True) - 1.0
    pair_of = iota((lane_dev, pairs), 1)
    owner = (pair_of // slots == iota((lane_dev, pairs), 0)).astype(BF16)
    tall = spread_out(partners_ref[...], owner)
    at_slot = iota((slots, pairs), 1) % slots == iota((slots, pairs), 0)
    target = jnp.sum(jnp.where(at_slot, tall, 0.0), axis=0, keepdims=True).astype(jnp.int32)
    pair_row = iota((1, pairs), 1)
    pick = (target == iota((lanes, pairs), 0)).astype(BF16)
    place = (
        (target // lane_dev) * lane_dev + pair_row // slots == iota((lanes, pairs), 0)
    ).astype(BF16)
    counted = nn(
        jnp.broadcast_to(counts_ref[...], (8, lane_dev)).astype(F32).astype(BF16), owner
    )[0:1]
    gain = jnp.where((pair_row % slots).astype(F32) < counted, F32(scale), 0.0)

    for off in list(range(1, n_rec)) + [0]:
        there = (rec + off) % n_rec
        first = there * lag_dev
        across = pl.ds(pl.multiple_of((first // HALF) * lanes, lanes), lanes)
        delay_at = first % HALF
        forward = jnp.zeros((lag_dev, lanes), F32)
        stack = []
        for m in range(lane_dev):
            rows = pl.ds(pl.multiple_of(m * HALF + delay_at, lag_dev), lag_dev)
            block = acc[rows, across]
            forward = jnp.where(mine == float(m), block, forward)
            stack.extend(pieces(block, 2))
        picked = nn(jnp.concatenate(stack, axis=0), pick)
        reverse = jnp.zeros((lag_dev, pairs), F32)
        for m in range(lane_dev):
            at = 2 * m * lag_dev
            both = picked[at : at + lag_dev] + picked[at + lag_dev : at + 2 * lag_dev]
            reverse = jnp.where(pair_row // slots == m, both, reverse)
        zbuf[off, :, 0:lanes] = forward
        zbuf[off, :, lanes : lanes + pairs] = reverse
        if off > 0:
            go(remote(zbuf.at[off], zin.at[off], send_z.at[off], recv_z.at[off], {"rec": there}))

    total = zbuf[0]
    for off in range(1, n_rec):
        remote(
            zbuf.at[off], zin.at[off], send_z.at[off], recv_z.at[off], {"lane": sibling}
        ).wait_recv()
        total += zin[off]

    line = (iota((lanes, lanes), 0) == iota((lanes, lanes), 1)).astype(BF16)
    forward_sum = total[:, 0:lanes]
    if lag_dev < 128:
        forward_sum = jnp.concatenate(
            [forward_sum, jnp.zeros((128 - lag_dev, lanes), F32)], axis=0
        )
    turned = jnp.zeros((lanes, 128), F32)
    for part in pieces(forward_sum, 3):
        turned += nt(line, part)
    fout[...] = turned
    fin[rows_of(me), :] = fout[rows_of(me), :]
    for off in range(1, n_lane):
        there = (me + off) % n_lane
        go(
            remote(
                fout.at[rows_of(there), :], fin.at[rows_of(me), :],
                send_f.at[off], recv_f.at[off], {"lane": there},
            )
        )
    out_ref[1] = total[:, lanes : lanes + pairs] * gain
    for off in range(1, n_lane):
        block = fin.at[rows_of((me + n_lane - off) % n_lane), :]
        remote(block, block, send_f.at[off], recv_f.at[off], {"lane": sibling}).wait_recv()
    back = (iota((lag_dev, 128), 0) == iota((lag_dev, 128), 1)).astype(BF16)
    final = jnp.zeros((lag_dev, pairs), F32)
    for part in pieces(fin[...], 3):
        final += nn(nt(back, part).astype(BF16), place)
    out_ref[0] = final * gain
    for copy in sent:
        copy.wait_send()


def per_device(waveforms, patterns, partners, counts):
    lane_dev, time_dev = waveforms.shape
    slots = partners.shape[1]
    n_lane, n_rec = lax.axis_size("lane"), lax.axis_size("rec")
    lanes, pairs = lane_dev * n_lane, lane_dev * slots
    n_z = n_lane // 2
    lag_dev = LAGS // n_rec
    chunks = 4
    scale = (5.0 * time_dev * n_rec) ** -0.5
    dma = pltpu.SemaphoreType.DMA
    return pl.pallas_call(
        functools.partial(kernel, n_lane, n_rec, scale, chunks),
        out_shape=jax.ShapeDtypeStruct((2, lag_dev, pairs), F32),
        in_specs=[pl.BlockSpec(memory_space=pltpu.HBM)] * 2
        + [pl.BlockSpec(memory_space=pltpu.VMEM)] * 2,
        out_specs=pl.BlockSpec(memory_space=pltpu.VMEM),
        scratch_shapes=[
            pltpu.VMEM((lanes, time_dev + 2 * HALF), BF16),
            pltpu.VMEM((lane_dev, time_dev), jnp.int32),
            pltpu.VMEM((lane_dev, time_dev + LAGS), F32),
            pltpu.VMEM((n_lane, slots, lanes), F32),
            pltpu.VMEM((lane_dev, LAGS), BF16),
            pltpu.VMEM((lane_dev, LAGS), BF16),
            pltpu.VMEM((lane_dev * HALF, time_dev + HALF), BF16),
            pltpu.VMEM((lane_dev * HALF, 2 * lanes), F32),
            pltpu.VMEM((n_rec, lag_dev, lanes + pairs), F32),
            pltpu.VMEM((n_rec, lag_dev, lanes + pairs), F32),
            pltpu.VMEM((lanes, 128), F32),
            pltpu.VMEM((lanes, 128), F32),
            dma((1,)), dma((1,)),
            dma((n_z, chunks)), dma((n_z, chunks)),
            dma((n_z, chunks)), dma((n_z, chunks)),
            dma((n_lane,)), dma((n_lane,)),
            dma((1,)), dma((1,)),
            dma((n_rec,)), dma((n_rec,)),
            dma((n_lane,)), dma((n_lane,)),
        ],
        compiler_params=pltpu.CompilerParams(
            collective_id=0, has_side_effects=True, vmem_limit_bytes=56 * 1024 * 1024
        ),
    )(waveforms, patterns, partners.T, counts[None, :])


def solution(mesh):
    in_specs = (P("lane", "rec"), P("lane", "rec"), P("lane", None), P("lane"))
    out_specs = P(None, "rec", "lane")
    return jax.shard_map(
        per_device, mesh=mesh, in_specs=in_specs, out_specs=out_specs, check_vma=False
    )
```

time: 39.4 us -> 41.3 us (1.048)
  Pallas kernels: 35.8 us -> 39.6 us
  local copies, waits for them, and re-layouts: 3.35 us -> 1.47 us
    pallas_call x1, Pallas kernels: 35.8 us -> 39.6 us  [per_device(): pl.pallas_call(functools.partial(kernel, n_lane, n_rec, scale, chunks), o...]
    unnamed x8 -> x1, local copies, waits for them, and re-layouts: 3.26 us -> 1.47 us
where the time goes in v2:
time: 41.3 us; the launch traced here: 41.1 us
  Pallas kernels  39.6 us (96%)
  local copies, waits for them, and re-layouts  1.47 us (4%)
    pallas_call x1, Pallas kernels, per_device(): pl.pallas_call(functools.partial(kernel, n_lane, n_rec, scale, chunks), o...  39.6 us
    unnamed x1, local copies, waits for them, and re-layouts  1.47 us

profile of v2, /device:TPU:0, one launch (start us, length us, event | category | flops | bytes accessed | tf_op | source)
XLA Modules:
  0.0 41.1 jit_solution(17404858098963137819)
XLA Ops:
  0.0 39.6 %shard_map.46 = f32[2,64,128]{2,1,0:T(8,128)} custom-call(bf16[16,4096]{1,0:T(8,128)(2,1)} %w_ref.1, s32[16,4096]{1,0:T(8,128)} %pat_ref.1, s32[8,16]{1,0:T(8,128)} %bitcast.2, s32[1,16]{1,0:T(1,128)} %bitcast.3), custom_call_target="tpu_custom_call" | custom-call | tf_op jit(solution)/shard_map/pallas_call | solution.py:287
  39.6 1.5 %copy.6 = f32[2,64,128]{2,1,0:T(8,128)} copy(f32[2,64,128]{2,1,0:T(8,128)} %shard_map.46) | data formatting | bytes 131072

commit v3 on v2

--- a/solution.py
+++ b/solution.py
@@ -9,6 +9,8 @@
 
 LAGS = 256
 HALF = 128
+FINE = 16
+STEPS = HALF // FINE
 MESH = pl.DeviceIdType.MESH
 F32 = jnp.float32
 BF16 = jnp.bfloat16
@@ -44,7 +46,7 @@
 def kernel(
     n_lane, n_rec, scale, chunks,
     w_ref, pat_ref, partners_ref, counts_ref, out_ref,
-    wall, pats, ext, named, rim, halo, delayed, acc, zbuf, zin, fout, fin,
+    wall, pats, named, rim, halo, shifted, refs, acc, zbuf, zin, fout, fin,
     local_w, local_p, send_d, recv_d, send_s, recv_s, send_m, recv_m, send_h, recv_h,
     send_z, recv_z, send_f, recv_f,
 ):
@@ -55,6 +57,7 @@
     n_z = n_lane // 2
     lag_dev = LAGS // n_rec
     wide = time_dev // chunks
+    cols = FINE * lane_dev
     me = lax.axis_index("lane")
     rec = lax.axis_index("rec")
     z, core = me // 2, me % 2
@@ -99,7 +102,6 @@
     named[0] = inside
     take_p.wait()
     levels = (2 * pats[...] - 3).astype(F32)
-    ext[:, LAGS : LAGS + time_dev] = levels
     rim[...] = levels[:, time_dev - LAGS :].astype(BF16)
 
     pl.semaphore_wait(barrier, n_lane - 1 + n_rec - 1)
@@ -135,44 +137,49 @@
             )
         )
 
+    unit = (iota((LAGS, LAGS), 0) == iota((LAGS, LAGS), 1)).astype(BF16)
+
+    def turn(b):
+        part = slice(b * LAGS, (b + 1) * LAGS)
+        refs[part, :] = nt(unit, shifted[:, part]).astype(BF16)
+
+    for r in range(FINE):
+        moved = levels if r == 0 else pltpu.roll(levels, r, 1)
+        shifted[r * lane_dev : (r + 1) * lane_dev, LAGS:] = moved.astype(BF16)
+    for b in range(2, time_dev // LAGS + 1):
+        turn(b)
     to_next.wait_recv()
-    ext[:, 0:LAGS] = jnp.where(rec > 0, halo[...].astype(F32), 0.0)
-
-    def width_of(c):
-        return wide + (HALF if c == chunks - 1 else 0)
-
-    def delay(c):
-        def body(m, carry):
-            row = ext[pl.ds(m, 1), c * wide : c * wide + width_of(c) + HALF]
-            same = jnp.broadcast_to(row, (HALF, width_of(c) + HALF))
-            moved = pltpu.roll(same, 0, 1, stride=1, stride_axis=0)
-            delayed[pl.ds(pl.multiple_of(m * HALF, HALF), HALF), c * wide : c * wide + width_of(c)] = (
-                moved[:, HALF:].astype(BF16)
-            )
+    before = jnp.where(rec > 0, halo[...].astype(F32), 0.0)
+    rest = jnp.concatenate([before, levels[:, 0:LAGS]], axis=1)
+    for r in range(FINE):
+        moved = rest if r == 0 else pltpu.roll(rest, r, 1)
+        shifted[r * lane_dev : (r + 1) * lane_dev, 0 : 2 * LAGS] = moved.astype(BF16)
+    for b in range(2):
+        turn(b)
+
+    def multiply(c):
+        begin = c * wide
+        width = wide + (HALF if c == chunks - 1 else 0)
+        group = 2
+
+        def body(step, carry):
+            first = wall[:, begin : begin + width]
+            second = wall[:, begin + HALF : begin + HALF + width]
+            rows = jnp.concatenate([first, second], axis=0)
+            for i in range(group):
+                a = step * group + i
+                start = pl.multiple_of(begin + HALF - FINE * a, FINE)
+                term = nn(rows, refs[pl.ds(start, width), :])
+                if c == 0:
+                    acc[a] = term
+                else:
+                    acc[a] += term
             return carry
 
-        lax.fori_loop(0, lane_dev, body, 0)
-
-    group = 4
-
-    def multiply(c):
-        def body(g, carry):
-            first = wall[:, c * wide : c * wide + width_of(c)]
-            second = wall[:, c * wide + HALF : c * wide + width_of(c) + HALF]
-            held = jnp.concatenate([first, second], axis=0)
-            rows = pl.ds(pl.multiple_of(g * group * HALF, group * HALF), group * HALF)
-            term = nt(delayed[rows, c * wide : c * wide + width_of(c)], held)
-            if c == 0:
-                acc[rows, :] = term
-            else:
-                acc[rows, :] += term
-            return carry
-
-        lax.fori_loop(0, lane_dev // group, body, 0)
+        lax.fori_loop(0, STEPS // group, body, 0)
 
     for c in range(chunks + 1):
         if c < chunks:
-            delay(c)
             for off in range(1, n_z):
                 block = wall.at[from_chip(off, True), span(c)]
                 remote(
@@ -196,14 +203,29 @@
         inside = inside + named[off]
     local = inside - 1.0 - (me * lane_dev).astype(F32)
     here = (local >= 0.0) & (local < float(lane_dev))
-    mine = jnp.sum(jnp.where(here, local + 1.0, 0.0), axis=0, keepdims=True) - 1.0
+    keep = jnp.where(here, local + 1.0, 0.0)
+
+    def turn_small(rows):
+        width = rows.shape[1]
+        same = (iota((width, width), 0) == iota((width, width), 1)).astype(BF16)
+        low, high = rows.astype(jnp.int32) % 64, rows.astype(jnp.int32) // 64
+        low, high = low.astype(F32).astype(BF16), high.astype(F32).astype(BF16)
+        column = jnp.sum(64.0 * nt(same, high) + nt(same, low), axis=1, keepdims=True)
+        return column.astype(jnp.int32)
+
+    mine = turn_small(keep) - 1
+    keep_forward = iota((lanes, cols), 1) % lane_dev == mine
     pair_of = iota((lane_dev, pairs), 1)
     owner = (pair_of // slots == iota((lane_dev, pairs), 0)).astype(BF16)
     tall = spread_out(partners_ref[...], owner)
     at_slot = iota((slots, pairs), 1) % slots == iota((slots, pairs), 0)
     target = jnp.sum(jnp.where(at_slot, tall, 0.0), axis=0, keepdims=True).astype(jnp.int32)
     pair_row = iota((1, pairs), 1)
-    pick = (target == iota((lanes, pairs), 0)).astype(BF16)
+    tall_column = turn_small(jnp.where(at_slot, tall, 0.0))
+    pick = (tall_column == iota((pairs, lanes), 1)).astype(BF16)
+    pick = jnp.concatenate([pick, pick], axis=1)
+    keep_reverse = iota((pairs, cols), 1) % lane_dev == iota((pairs, cols), 0) // slots
+    gather = (iota((FINE, cols), 1) // lane_dev == iota((FINE, cols), 0)).astype(BF16)
     place = (
         (target // lane_dev) * lane_dev + pair_row // slots == iota((lanes, pairs), 0)
     ).astype(BF16)
@@ -214,24 +236,24 @@
 
     for off in list(range(1, n_rec)) + [0]:
         there = (rec + off) % n_rec
-        first = there * lag_dev
-        across = pl.ds(pl.multiple_of((first // HALF) * lanes, lanes), lanes)
-        delay_at = first % HALF
-        forward = jnp.zeros((lag_dev, lanes), F32)
-        stack = []
-        for m in range(lane_dev):
-            rows = pl.ds(pl.multiple_of(m * HALF + delay_at, lag_dev), lag_dev)
-            block = acc[rows, across]
-            forward = jnp.where(mine == float(m), block, forward)
-            stack.extend(pieces(block, 2))
-        picked = nn(jnp.concatenate(stack, axis=0), pick)
-        reverse = jnp.zeros((lag_dev, pairs), F32)
-        for m in range(lane_dev):
-            at = 2 * m * lag_dev
-            both = picked[at : at + lag_dev] + picked[at + lag_dev : at + 2 * lag_dev]
-            reverse = jnp.where(pair_row // slots == m, both, reverse)
-        zbuf[off, :, 0:lanes] = forward
-        zbuf[off, :, lanes : lanes + pairs] = reverse
+        count = lag_dev // FINE
+        first = there * count
+        rows = pl.ds(pl.multiple_of((first // STEPS) * lanes, lanes), lanes)
+        blocks = [acc[first % STEPS + i, rows, :] for i in range(count)]
+        kept = [jnp.where(keep_forward, block, 0.0) for block in blocks]
+        split = [jnp.concatenate(pieces(block, 2), axis=0) for block in blocks]
+        picked = nn(pick, jnp.concatenate(split, axis=1))
+        for i in range(count):
+            kept.append(jnp.where(keep_reverse, picked[:, i * cols : (i + 1) * cols], 0.0))
+        kept = jnp.concatenate(kept, axis=0)
+        summed = jnp.zeros((FINE, kept.shape[0]), F32)
+        for part in pieces(kept, 2):
+            summed += nt(gather, part)
+        for i in range(count):
+            at = slice(i * FINE, (i + 1) * FINE)
+            zbuf[off, at, 0:lanes] = summed[:, i * lanes : (i + 1) * lanes]
+            begin = count * lanes + i * pairs
+            zbuf[off, at, lanes : lanes + pairs] = summed[:, begin : begin + pairs]
         if off > 0:
             go(remote(zbuf.at[off], zin.at[off], send_z.at[off], recv_z.at[off], {"rec": there}))
 
@@ -281,6 +303,7 @@
     lanes, pairs = lane_dev * n_lane, lane_dev * slots
     n_z = n_lane // 2
     lag_dev = LAGS // n_rec
+    cols = FINE * lane_dev
     chunks = 4
     scale = (5.0 * time_dev * n_rec) ** -0.5
     dma = pltpu.SemaphoreType.DMA
@@ -293,12 +316,12 @@
         scratch_shapes=[
             pltpu.VMEM((lanes, time_dev + 2 * HALF), BF16),
             pltpu.VMEM((lane_dev, time_dev), jnp.int32),
-            pltpu.VMEM((lane_dev, time_dev + LAGS), F32),
             pltpu.VMEM((n_lane, slots, lanes), F32),
             pltpu.VMEM((lane_dev, LAGS), BF16),
             pltpu.VMEM((lane_dev, LAGS), BF16),
-            pltpu.VMEM((lane_dev * HALF, time_dev + HALF), BF16),
-            pltpu.VMEM((lane_dev * HALF, 2 * lanes), F32),
+            pltpu.VMEM((cols, time_dev + LAGS), BF16),
+            pltpu.VMEM((time_dev + LAGS, cols), BF16),
+            pltpu.VMEM((STEPS, 2 * lanes, cols), F32),
             pltpu.VMEM((n_rec, lag_dev, lanes + pairs), F32),
             pltpu.VMEM((n_rec, lag_dev, lanes + pairs), F32),
             pltpu.VMEM((lanes, 128), F32),

time: 41.3 us -> 38.2 us (0.925)
  Pallas kernels: 39.6 us -> 36.5 us
    pallas_call x1, Pallas kernels: 39.6 us -> 36.5 us  [per_device(): pl.pallas_call(functools.partial(kernel, n_lane, n_rec, scale, chunks), o...]
where the time goes in v3:
time: 38.2 us; the launch traced here: 38 us
  Pallas kernels  36.5 us (96%)
  local copies, waits for them, and re-layouts  1.47 us (4%)
    pallas_call x1, Pallas kernels, per_device(): pl.pallas_call(functools.partial(kernel, n_lane, n_rec, scale, chunks), o...  36.5 us
    unnamed x1, local copies, waits for them, and re-layouts  1.47 us

profile of v3, /device:TPU:0, one launch (start us, length us, event | category | flops | bytes accessed | tf_op | source)
XLA Modules:
  0.0 38.0 jit_solution(16850672277463815730)
XLA Ops:
  0.0 36.5 %shard_map.46 = f32[2,64,128]{2,1,0:T(8,128)} custom-call(bf16[16,4096]{1,0:T(8,128)(2,1)} %w_ref.1, s32[16,4096]{1,0:T(8,128)} %pat_ref.1, s32[8,16]{1,0:T(8,128)} %bitcast.2, s32[1,16]{1,0:T(1,128)} %bitcast.3), custom_call_target="tpu_custom_call" | custom-call | tf_op jit(solution)/shard_map/pallas_call | solution.py:310
  36.5 1.5 %copy.6 = f32[2,64,128]{2,1,0:T(8,128)} copy(f32[2,64,128]{2,1,0:T(8,128)} %shard_map.46) | data formatting | bytes 131072

commit v4 on v3

--- a/solution.py
+++ b/solution.py
@@ -114,6 +114,13 @@
 
     to_next = remote(rim, halo, send_h.at[0], recv_h.at[0], {"rec": (rec + 1) % n_rec})
     go(to_next)
+    for off in range(1, n_lane):
+        go(
+            remote(
+                named.at[0], named.at[off], send_m.at[off], recv_m.at[off],
+                {"lane": (me + off) % n_lane},
+            )
+        )
     for c in range(chunks):
         part = w_ref.at[:, pl.ds(c * wide, wide)]
         for off in range(1, n_z):
@@ -129,14 +136,6 @@
                 {"lane": sibling},
             )
         )
-    for off in range(1, n_lane):
-        go(
-            remote(
-                named.at[0], named.at[off], send_m.at[off], recv_m.at[off],
-                {"lane": (me + off) % n_lane},
-            )
-        )
-
     unit = (iota((LAGS, LAGS), 0) == iota((LAGS, LAGS), 1)).astype(BF16)
 
     def turn(b):
@@ -156,45 +155,6 @@
         shifted[r * lane_dev : (r + 1) * lane_dev, 0 : 2 * LAGS] = moved.astype(BF16)
     for b in range(2):
         turn(b)
-
-    def multiply(c):
-        begin = c * wide
-        width = wide + (HALF if c == chunks - 1 else 0)
-        group = 2
-
-        def body(step, carry):
-            first = wall[:, begin : begin + width]
-            second = wall[:, begin + HALF : begin + HALF + width]
-            rows = jnp.concatenate([first, second], axis=0)
-            for i in range(group):
-                a = step * group + i
-                start = pl.multiple_of(begin + HALF - FINE * a, FINE)
-                term = nn(rows, refs[pl.ds(start, width), :])
-                if c == 0:
-                    acc[a] = term
-                else:
-                    acc[a] += term
-            return carry
-
-        lax.fori_loop(0, STEPS // group, body, 0)
-
-    for c in range(chunks + 1):
-        if c < chunks:
-            for off in range(1, n_z):
-                block = wall.at[from_chip(off, True), span(c)]
-                remote(
-                    block, block, send_d.at[off, c], recv_d.at[off, c], {"lane": sibling}
-                ).wait_recv()
-                go(remote(block, block, send_s.at[off, c], recv_s.at[off, c], {"lane": sibling}))
-        if c == 1:
-            take_w.wait()
-        if c > 0:
-            for off in range(n_z):
-                block = wall.at[from_chip(off, False), span(c - 1)]
-                remote(
-                    block, block, send_s.at[off, c - 1], recv_s.at[off, c - 1], {"lane": sibling}
-                ).wait_recv()
-            multiply(c - 1)
 
     for off in range(1, n_lane):
         remote(
@@ -233,6 +193,45 @@
         jnp.broadcast_to(counts_ref[...], (8, lane_dev)).astype(F32).astype(BF16), owner
     )[0:1]
     gain = jnp.where((pair_row % slots).astype(F32) < counted, F32(scale), 0.0)
+
+    def multiply(c):
+        begin = c * wide
+        width = wide + (HALF if c == chunks - 1 else 0)
+        group = 2
+
+        def body(step, carry):
+            first = wall[:, begin : begin + width]
+            second = wall[:, begin + HALF : begin + HALF + width]
+            rows = jnp.concatenate([first, second], axis=0)
+            for i in range(group):
+                a = step * group + i
+                start = pl.multiple_of(begin + HALF - FINE * a, FINE)
+                term = nn(rows, refs[pl.ds(start, width), :])
+                if c == 0:
+                    acc[a] = term
+                else:
+                    acc[a] += term
+            return carry
+
+        lax.fori_loop(0, STEPS // group, body, 0)
+
+    for c in range(chunks + 1):
+        if c < chunks:
+            for off in range(1, n_z):
+                block = wall.at[from_chip(off, True), span(c)]
+                remote(
+                    block, block, send_d.at[off, c], recv_d.at[off, c], {"lane": sibling}
+                ).wait_recv()
+                go(remote(block, block, send_s.at[off, c], recv_s.at[off, c], {"lane": sibling}))
+        if c == 1:
+            take_w.wait()
+        if c > 0:
+            for off in range(n_z):
+                block = wall.at[from_chip(off, False), span(c - 1)]
+                remote(
+                    block, block, send_s.at[off, c - 1], recv_s.at[off, c - 1], {"lane": sibling}
+                ).wait_recv()
+            multiply(c - 1)
 
     for off in list(range(1, n_rec)) + [0]:
         there = (rec + off) % n_rec
@@ -264,16 +263,12 @@
         ).wait_recv()
         total += zin[off]
 
-    line = (iota((lanes, lanes), 0) == iota((lanes, lanes), 1)).astype(BF16)
     forward_sum = total[:, 0:lanes]
     if lag_dev < 128:
         forward_sum = jnp.concatenate(
             [forward_sum, jnp.zeros((128 - lag_dev, lanes), F32)], axis=0
         )
-    turned = jnp.zeros((lanes, 128), F32)
-    for part in pieces(forward_sum, 3):
-        turned += nt(line, part)
-    fout[...] = turned
+    fout[...] = forward_sum.T
     fin[rows_of(me), :] = fout[rows_of(me), :]
     for off in range(1, n_lane):
         there = (me + off) % n_lane
@@ -287,10 +282,9 @@
     for off in range(1, n_lane):
         block = fin.at[rows_of((me + n_lane - off) % n_lane), :]
         remote(block, block, send_f.at[off], recv_f.at[off], {"lane": sibling}).wait_recv()
-    back = (iota((lag_dev, 128), 0) == iota((lag_dev, 128), 1)).astype(BF16)
-    final = jnp.zeros((lag_dev, pairs), F32)
-    for part in pieces(fin[...], 3):
-        final += nn(nt(back, part).astype(BF16), place)
+    returned = fin[...].T[0:lag_dev]
+    placed = nn(jnp.concatenate(pieces(returned, 3), axis=0), place)
+    final = placed[0:lag_dev] + placed[lag_dev : 2 * lag_dev] + placed[2 * lag_dev :]
     out_ref[0] = final * gain
     for copy in sent:
         copy.wait_send()
@@ -335,7 +329,7 @@
             dma((n_lane,)), dma((n_lane,)),
         ],
         compiler_params=pltpu.CompilerParams(
-            collective_id=0, has_side_effects=True, vmem_limit_bytes=56 * 1024 * 1024
+            collective_id=0, has_side_effects=True, vmem_limit_bytes=(256 + lanes) * 64 * 1024
         ),
     )(waveforms, patterns, partners.T, counts[None, :])
 

time: 38.2 us -> 38.6 us (1.010)
  local copies, waits for them, and re-layouts: 1.47 us -> 3.83 us
  Pallas kernels: 36.5 us -> 34.6 us
    unnamed x1 -> x9, local copies, waits for them, and re-layouts: 1.47 us -> 3.83 us
    pallas_call x1, Pallas kernels: 36.5 us -> 34.6 us  [per_device(): pl.pallas_call(functools.partial(kernel, n_lane, n_rec, scale, chunks), o...]
where the time goes in v4:
time: 38.6 us; the launch traced here: 38.4 us
  Pallas kernels  34.6 us (90%)
  local copies, waits for them, and re-layouts  3.83 us (10%)
    pallas_call x1, Pallas kernels, per_device(): pl.pallas_call(functools.partial(kernel, n_lane, n_rec, scale, chunks), o...  34.6 us
    unnamed x9, local copies, waits for them, and re-layouts  3.83 us

profile of v4, /device:TPU:0, one launch (start us, length us, event | category | flops | bytes accessed | tf_op | source)
XLA Modules:
  0.0 38.4 jit_solution(5049280928665159322)
XLA Ops:
  0.0 0.0 copy-start.3
  0.0 0.7 %copy-done.3 = s32[16]{0:T(128)S(1)} copy-done((s32[16]{0:T(128)S(1)}, s32[16]{0:T(128)}, u32[]{:S(2)}) %copy-start.3) | copy-done | bytes 88
  0.7 0.0 copy-start
  0.7 0.9 %copy-done = s32[16,4096]{1,0:T(8,128)S(1)} copy-done((s32[16,4096]{1,0:T(8,128)S(1)}, s32[16,4096]{1,0:T(8,128)}, u32[]{:S(2)}) %copy-start) | copy-done | bytes 262168
  1.6 0.0 copy-start.1
  1.6 0.9 %copy-done.1 = bf16[16,4096]{1,0:T(8,128)(2,1)S(1)} copy-done((bf16[16,4096]{1,0:T(8,128)(2,1)S(1)}, bf16[16,4096]{1,0:T(8,128)(2,1)}, u32[]{:S(2)}) %copy-start.1) | copy-done | bytes 131096
  2.5 0.0 copy-start.2
  2.5 0.7 %copy-done.2 = s32[16,8]{0,1:T(8,128)S(1)} copy-done((s32[16,8]{0,1:T(8,128)S(1)}, s32[16,8]{0,1:T(8,128)}, u32[]{:S(2)}) %copy-start.2) | copy-done | bytes 536
  3.2 34.6 %shard_map.46 = f32[2,64,128]{2,1,0:T(8,128)S(1)} custom-call(bf16[16,4096]{1,0:T(8,128)(2,1)S(1)} %copy-done.1, s32[16,4096]{1,0:T(8,128)S(1)} %copy-done, s32[8,16]{1,0:T(8,128)S(1)} %bitcast.2, s32[1,16]{1,0:T(1,128)S(1)} %bitcast.3), custom_call_target="tpu_custom_call" | custom-call | tf_op jit(solution)/shard_map/pallas_call | solution.py:304
  37.8 0.6 %copy.6 = f32[2,64,128]{2,1,0:T(8,128)} copy(f32[2,64,128]{2,1,0:T(8,128)S(1)} %shard_map.46) | data formatting | bytes 131072
Async XLA Ops:
  0.0 0.7 %copy-start.3 = (s32[16]{0:T(128)S(1)}, s32[16]{0:T(128)}, u32[]{:S(2)}) copy-start(s32[16]{0:T(128)} %param.7) | copy-start | bytes 196
  0.7 0.9 %copy-start = (s32[16,4096]{1,0:T(8,128)S(1)}, s32[16,4096]{1,0:T(8,128)}, u32[]{:S(2)}) copy-start(s32[16,4096]{1,0:T(8,128)} %pat_ref.1) | copy-start | bytes 786436
  1.6 0.9 %copy-start.1 = (bf16[16,4096]{1,0:T(8,128)(2,1)S(1)}, bf16[16,4096]{1,0:T(8,128)(2,1)}, u32[]{:S(2)}) copy-start(bf16[16,4096]{1,0:T(8,128)(2,1)} %w_ref.1) | copy-start | bytes 393220
  2.5 0.7 %copy-start.2 = (s32[16,8]{0,1:T(8,128)S(1)}, s32[16,8]{0,1:T(8,128)}, u32[]{:S(2)}) copy-start(s32[16,8]{0,1:T(8,128)} %param.6) | copy-start | bytes 1540

commit v5 on v4

--- a/solution.py
+++ b/solution.py
@@ -85,9 +85,6 @@
     def span(c):
         return pl.ds(HALF + c * wide, wide)
 
-    def from_chip(off, same):
-        return rows_of(2 * ((z + n_z - off) % n_z) + (core if same else 1 - core))
-
     take_p = pltpu.make_async_copy(pat_ref, pats, local_p.at[0])
     take_p.start()
     take_w = pltpu.make_async_copy(
@@ -121,21 +118,40 @@
                 {"lane": (me + off) % n_lane},
             )
         )
+    def block_of(chip, same, c):
+        owner = 2 * chip + (core if same else 1 - core)
+        return wall.at[rows_of(jnp.clip(owner, 0, n_lane - 1)), span(c)]
+
+    def on_line(chip):
+        return (chip >= 0) & (chip < n_z)
+
+    def passed(d, side, c, first=False):
+        way = 1 - 2 * side
+        target = wall.at[rows_of(me), span(c)] if first else block_of(z - way * (d - 1), True, c)
+        source = w_ref.at[:, pl.ds(c * wide, wide)] if first else target
+        return remote(
+            source, target, send_d.at[d, side, c], recv_d.at[d, side, c],
+            {"lane": jnp.clip(2 * (z + way) + core, 0, n_lane - 1)},
+        )
+
+    def across(d, side, c, same=True):
+        block = block_of(z - (1 - 2 * side) * d, same, c)
+        return remote(
+            block, block, send_s.at[d, side, c], recv_s.at[d, side, c], {"lane": sibling}
+        )
+
+    def own_across(c):
+        return remote(
+            w_ref.at[:, pl.ds(c * wide, wide)], wall.at[rows_of(me), span(c)],
+            send_s.at[0, 0, c], recv_s.at[0, 0, c], {"lane": sibling},
+        )
+
     for c in range(chunks):
-        part = w_ref.at[:, pl.ds(c * wide, wide)]
-        for off in range(1, n_z):
-            go(
-                remote(
-                    part, wall.at[rows_of(me), span(c)], send_d.at[off, c], recv_d.at[off, c],
-                    {"lane": 2 * ((z + off) % n_z) + core},
-                )
-            )
-        go(
-            remote(
-                part, wall.at[rows_of(me), span(c)], send_s.at[0, c], recv_s.at[0, c],
-                {"lane": sibling},
-            )
-        )
+        for side in range(2):
+            @pl.when(on_line(z + 1 - 2 * side))
+            def _():
+                passed(1, side, c, True).start()
+        own_across(c).start()
     unit = (iota((LAGS, LAGS), 0) == iota((LAGS, LAGS), 1)).astype(BF16)
 
     def turn(b):
@@ -215,23 +231,42 @@
 
         lax.fori_loop(0, STEPS // group, body, 0)
 
-    for c in range(chunks + 1):
-        if c < chunks:
-            for off in range(1, n_z):
-                block = wall.at[from_chip(off, True), span(c)]
+    def relay(d, c):
+        for side in range(2):
+            way = 1 - 2 * side
+
+            @pl.when(on_line(z - way * d))
+            def _():
+                block = block_of(z - way * d, True, c)
                 remote(
-                    block, block, send_d.at[off, c], recv_d.at[off, c], {"lane": sibling}
+                    block, block, send_d.at[d, side, c], recv_d.at[d, side, c],
+                    {"lane": sibling},
                 ).wait_recv()
-                go(remote(block, block, send_s.at[off, c], recv_s.at[off, c], {"lane": sibling}))
-        if c == 1:
+                across(d, side, c).start()
+
+            if d + 1 < n_z:
+                @pl.when(on_line(z - way * d) & on_line(z + way))
+                def _():
+                    passed(d + 1, side, c).start()
+
+    def complete(c):
+        across(0, 0, c, False).wait_recv()
+        for d in range(1, n_z):
+            for side in range(2):
+                @pl.when(on_line(z - (1 - 2 * side) * d))
+                def _():
+                    across(d, side, c, False).wait_recv()
+
+    for slot in range(chunks + n_z - 1):
+        for d in range(1, n_z):
+            if 0 <= slot + 1 - d < chunks:
+                relay(d, slot + 1 - d)
+        c = slot + 1 - n_z
+        if c == 0:
             take_w.wait()
-        if c > 0:
-            for off in range(n_z):
-                block = wall.at[from_chip(off, False), span(c - 1)]
-                remote(
-                    block, block, send_s.at[off, c - 1], recv_s.at[off, c - 1], {"lane": sibling}
-                ).wait_recv()
-            multiply(c - 1)
+        if c >= 0:
+            complete(c)
+            multiply(c)
 
     for off in list(range(1, n_rec)) + [0]:
         there = (rec + off) % n_rec
@@ -288,6 +323,24 @@
     out_ref[0] = final * gain
     for copy in sent:
         copy.wait_send()
+    for c in range(chunks):
+        own_across(c).wait_send()
+        for side in range(2):
+            way = 1 - 2 * side
+
+            @pl.when(on_line(z + way))
+            def _():
+                passed(1, side, c, True).wait_send()
+
+            for d in range(1, n_z):
+                @pl.when(on_line(z - way * d))
+                def _():
+                    across(d, side, c).wait_send()
+
+                if d + 1 < n_z:
+                    @pl.when(on_line(z - way * d) & on_line(z + way))
+                    def _():
+                        passed(d + 1, side, c).wait_send()
 
 
 def per_device(waveforms, patterns, partners, counts):
@@ -321,8 +374,8 @@
             pltpu.VMEM((lanes, 128), F32),
             pltpu.VMEM((lanes, 128), F32),
             dma((1,)), dma((1,)),
-            dma((n_z, chunks)), dma((n_z, chunks)),
-            dma((n_z, chunks)), dma((n_z, chunks)),
+            dma((n_z, 2, chunks)), dma((n_z, 2, chunks)),
+            dma((n_z, 2, chunks)), dma((n_z, 2, chunks)),
             dma((n_lane,)), dma((n_lane,)),
             dma((1,)), dma((1,)),
             dma((n_rec,)), dma((n_rec,)),

time: 38.6 us -> 39.1 us (1.013)
  Pallas kernels: 34.6 us -> 35 us
    pallas_call x1, Pallas kernels: 34.6 us -> 35 us  [per_device(): pl.pallas_call(functools.partial(kernel, n_lane, n_rec, scale, chunks), o...]
where the time goes in v5:
time: 39.1 us; the launch traced here: 38.9 us
  Pallas kernels  35 us (90%)
  local copies, waits for them, and re-layouts  3.83 us (10%)
    pallas_call x1, Pallas kernels, per_device(): pl.pallas_call(functools.partial(kernel, n_lane, n_rec, scale, chunks), o...  35 us
    unnamed x9, local copies, waits for them, and re-layouts  3.83 us

profile of v5, /device:TPU:0, one launch (start us, length us, event | category | flops | bytes accessed | tf_op | source)
XLA Modules:
  0.0 38.9 jit_solution(12993348585304795926)
XLA Ops:
  0.0 0.0 copy-start.3
  0.0 0.7 %copy-done.3 = s32[16]{0:T(128)S(1)} copy-done((s32[16]{0:T(128)S(1)}, s32[16]{0:T(128)}, u32[]{:S(2)}) %copy-start.3) | copy-done | bytes 88
  0.7 0.0 copy-start
  0.7 0.9 %copy-done = s32[16,4096]{1,0:T(8,128)S(1)} copy-done((s32[16,4096]{1,0:T(8,128)S(1)}, s32[16,4096]{1,0:T(8,128)}, u32[]{:S(2)}) %copy-start) | copy-done | bytes 262168
  1.6 0.0 copy-start.1
  1.6 0.9 %copy-done.1 = bf16[16,4096]{1,0:T(8,128)(2,1)S(1)} copy-done((bf16[16,4096]{1,0:T(8,128)(2,1)S(1)}, bf16[16,4096]{1,0:T(8,128)(2,1)}, u32[]{:S(2)}) %copy-start.1) | copy-done | bytes 131096
  2.5 0.0 copy-start.2
  2.5 0.7 %copy-done.2 = s32[16,8]{0,1:T(8,128)S(1)} copy-done((s32[16,8]{0,1:T(8,128)S(1)}, s32[16,8]{0,1:T(8,128)}, u32[]{:S(2)}) %copy-start.2) | copy-done | bytes 536
  3.2 35.0 %shard_map.46 = f32[2,64,128]{2,1,0:T(8,128)S(1)} custom-call(bf16[16,4096]{1,0:T(8,128)(2,1)S(1)} %copy-done.1, s32[16,4096]{1,0:T(8,128)S(1)} %copy-done, s32[8,16]{1,0:T(8,128)S(1)} %bitcast.2, s32[1,16]{1,0:T(1,128)S(1)} %bitcast.3), custom_call_target="tpu_custom_call" | custom-call | tf_op jit(solution)/shard_map/pallas_call | solution.py:357
  38.3 0.6 %copy.6 = f32[2,64,128]{2,1,0:T(8,128)} copy(f32[2,64,128]{2,1,0:T(8,128)S(1)} %shard_map.46) | data formatting | bytes 131072
Async XLA Ops:
  0.0 0.7 %copy-start.3 = (s32[16]{0:T(128)S(1)}, s32[16]{0:T(128)}, u32[]{:S(2)}) copy-start(s32[16]{0:T(128)} %param.7) | copy-start | bytes 196
  0.7 0.9 %copy-start = (s32[16,4096]{1,0:T(8,128)S(1)}, s32[16,4096]{1,0:T(8,128)}, u32[]{:S(2)}) copy-start(s32[16,4096]{1,0:T(8,128)} %pat_ref.1) | copy-start | bytes 786436
  1.6 0.9 %copy-start.1 = (bf16[16,4096]{1,0:T(8,128)(2,1)S(1)}, bf16[16,4096]{1,0:T(8,128)(2,1)}, u32[]{:S(2)}) copy-start(bf16[16,4096]{1,0:T(8,128)(2,1)} %w_ref.1) | copy-start | bytes 393220
  2.5 0.7 %copy-start.2 = (s32[16,8]{0,1:T(8,128)S(1)}, s32[16,8]{0,1:T(8,128)}, u32[]{:S(2)}) copy-start(s32[16,8]{0,1:T(8,128)} %param.6) | copy-start | bytes 1540
